TPU v7x, 32 devices: a whole 2x2x4 slice. The times are simulated.
32 devices in a mesh: row: 8 (over z, y), col: 4 (over x, core).
Axes of the slice: x: 2, y: 2, z: 4, core: 2. Of those that a mesh axis runs over, the one named last changes fastest.
Arguments:
- features: bfloat16 [4096, 256], P(('col', 'row')), may hold values from -6 to 6
- tile_values: bfloat16 [8, 4, 32, 128, 128], P('row', 'col'), may hold values from -0.125 to 0.125
- tile_rows: int32 [8, 4, 32], P('row', 'col'), may hold values from 0 to 3
- tile_cols: int32 [8, 4, 32], P('row', 'col'), may hold values from 0 to 7
- live_slots: int32 [8, 4], P('row', 'col'), may hold values from 4 to 32, as said below
- weight: bfloat16 [256, 256], replicated, may hold values from -0.375 to 0.375
- bias_vector: float32 [256], replicated, may hold values from -3 to 3
- cotangent: bfloat16 [4096, 256], P(('row', 'col')), may hold values from -6 to 6
Outputs:
- output: bfloat16 [4096, 256], P(('row', 'col'))
- grad_features: float32 [4096, 256], P(('col', 'row'))
- grad_weight: float32 [256, 256], replicated
Inputs may be any that keep to these rules, and one draw needn't show every extreme that they name: `live_slots`: some block uses all 32 slots.
All inputs are finite; a program needn't handle non-finite values.
Results may differ from a plain program's by a relative error of at most 0.0058.
Values may be sent and summed in bfloat16 or wider, within the bound.
A program may use at most 64 MiB of HBM per device.

v0:
```python
import jax
import jax.numpy as jnp
from jax import lax
from jax.sharding import PartitionSpec as P


def tile_products(tiles, picked, forward):
    if forward:
        return jnp.einsum("sab,sbf->saf", tiles, picked, preferred_element_type=jnp.float32)
    return jnp.einsum("sab,saf->sbf", tiles, picked, preferred_element_type=jnp.float32)


def place(products, target_ids, valid, target_count):
    one_hot = ((target_ids[:, None] == jnp.arange(target_count)[None, :]) & valid[:, None]).astype(
        jnp.float32
    )
    return jnp.einsum("sr,saf->raf", one_hot, products, precision=lax.Precision.HIGHEST)


def reduce_weight(local_weight):
    return lax.psum(local_weight, ("row", "col"))


def shards(features, tile_values, tile_rows, tile_cols, live_slots, weight, bias_vector, cotangent):
    tile_block = tile_values[0, 0]
    row_ids = tile_rows[0, 0]
    col_ids = tile_cols[0, 0]
    live_count = live_slots[0, 0]
    slot_count = tile_block.shape[0]
    tile_size = tile_block.shape[1]
    feature_width = features.shape[1]
    slot_index = jnp.arange(slot_count)
    valid = slot_index < live_count
    column_block = lax.all_gather(features, "row", axis=0, tiled=True)
    column_count = column_block.shape[0] // tile_size
    column_tiles = column_block.reshape(column_count, tile_size, feature_width)
    row_count = lax.axis_size("col") * features.shape[0] // tile_size
    partial_value = place(
        tile_products(tile_block, column_tiles[col_ids], True), row_ids, valid, row_count
    )
    summed = lax.psum_scatter(
        partial_value.reshape(row_count * tile_size, feature_width),
        "col",
        scatter_dimension=0,
        tiled=True,
    )
    aggregate = summed.astype(jnp.bfloat16)
    preact = jnp.dot(aggregate, weight, preferred_element_type=jnp.float32) + bias_vector
    sigmoid_z = jax.nn.sigmoid(preact)
    output = (preact * sigmoid_z).astype(jnp.bfloat16)
    grad_pre = (
        cotangent.astype(jnp.float32) * sigmoid_z * (1.0 + preact * (1.0 - sigmoid_z))
    ).astype(jnp.bfloat16)
    grad_aggregate = jnp.dot(grad_pre, weight.T, preferred_element_type=jnp.float32).astype(
        jnp.bfloat16
    )
    local_weight = lax.dot_general(
        aggregate, grad_pre, (((0,), (0,)), ((), ())), preferred_element_type=jnp.float32
    )
    row_block = lax.all_gather(grad_aggregate, "col", axis=0, tiled=True)
    row_tiles = row_block.reshape(row_count, tile_size, feature_width)
    partial_grad = place(
        tile_products(tile_block, row_tiles[row_ids], False), col_ids, valid, column_count
    )
    grad_features = lax.psum_scatter(
        partial_grad.reshape(column_count * tile_size, feature_width),
        "row",
        scatter_dimension=0,
        tiled=True,
    )
    grad_weight = reduce_weight(local_weight)
    return (output, grad_features, grad_weight)


def solution(mesh):
    return jax.shard_map(
        shards,
        mesh=mesh,
        in_specs=(
            P(("col", "row"), None),
            P("row", "col", None, None, None),
            P("row", "col", None),
            P("row", "col", None),
            P("row", "col"),
            P(),
            P(),
            P(("row", "col"), None),
        ),
        out_specs=(P(("row", "col"), None), P(("col", "row"), None), P()),
        check_vma=False,
    )
```

profile of v0, /device:TPU:0, one launch (start us, length us, event | category | flops | bytes accessed | tf_op | source)
XLA Modules:
  0.0 288.3 jit_solution(10860282830867920279)
XLA Ops:
  7.2 0.0 copy-start
  7.2 0.0 reduce-scatter.3.cloned.1.call-start
  8.0 0.7 fusion.21
  8.6 33.2 %all_gather.6 = bf16[1024,256]{1,0:T(8,128)(2,1)S(1)} all-gather(bf16[128,256]{1,0:T(8,128)(2,1)} %param.8), channel_id=1, replica_groups=mesh['row'=8,'col'=4] {'row'}, dimensions={0}, use_global_device_ids=true | all-gather | bytes 589824 | tf_op jit(solution)/shard_map/all_gather | solution.py:34
  41.8 2.0 gather_fusion
  43.8 0.0 copy-done
  43.8 4.3 %fusion.6 = f32[32,256,128]{2,1,0:T(8,128)} fusion(bf16[32,128,256]{2,1,0:T(8,128)(2,1)} %gather_fusion, bf16[1,1,32,128,128]{4,3,2,1,0:T(8,128)(2,1)S(1)} %copy-done), kind=kOutput, calls=%fused_computation.10 | convolution fusion | flops 268435456 | bytes 7340032 | tf_op jit(solution)/shard_map/sab,sbf->saf/dot_general | solution.py:9
  48.1 0.0 copy-start.1
  48.1 5.5 %copy.13 = f32[32,256,128]{1,0,2:T(8,128)} copy(f32[32,256,128]{2,1,0:T(8,128)} %fusion.6) | data formatting | bytes 8388608 | tf_op jit(solution)/shard_map/sab,sbf->saf/dot_general | solution.py:9
  53.6 0.0 copy-done.1
  53.6 0.0 copy-start.3
  53.6 0.0 copy-start.5
  53.6 3.7 %fusion.2 = f32[4,128,256]{2,0,1:T(4,128)S(1)} fusion(f32[32,256,128]{1,0,2:T(8,128)} %copy.13, s32[32]{0:T(128)S(1)} %bitcast.41, pred[32]{0:T(512)(128)(4,1)S(1)} %iota_compare_fusion.2), kind=kOutput, calls=%fused_computation.4 | convolution fusion | flops 50331904 | bytes 4718752 | tf_op jit(solution)/shard_map/sr,saf->raf/dot_general | solution.py:17
  57.3 0.0 copy-start.4
  57.3 0.9 copy.11
  58.2 0.0 reduce-scatter.3.cloned.1.call-update
  58.3 0.0 all-reduce.2.cloned.1.call-start
  58.3 22.8 %reduce-scatter.3.cloned.1.call-done = f32[128,256]{1,0:T(8,128)} async-done(((f32[512,256]{1,0:T(8,128)}), f32[128,256]{1,0:T(8,128)}) %reduce-scatter.3.cloned.1.call-update) | async-done | bytes 131088 | tf_op jit(solution)/shard_map/reduce_scatter | solution.py:41
  81.2 0.0 copy-done.3
  81.2 0.0 copy-done.5
  81.2 1.7 multiply_convert_fusion.1
  82.9 0.0 copy-done.4
  82.9 0.2 convolution_convert_fusion
  83.1 1.8 fusion.8
  85.0 0.0 all-reduce.2.cloned.1.call-update
  85.0 0.0 reduce-scatter.5.cloned.1.call-start
  85.0 5.8 %all_gather.7 = bf16[512,256]{1,0:T(8,128)(2,1)S(1)} all-gather(bf16[128,256]{1,0:T(8,128)(2,1)S(1)} %convolution_convert_fusion), channel_id=1, replica_groups=mesh['row'=8,'col'=4] {'col'}, dimensions={0}, use_global_device_ids=true | all-gather | bytes 327680 | tf_op jit(solution)/shard_map/all_gather | solution.py:60
  90.8 0.7 gather_fusion.1
  91.5 2.7 fusion.4
  94.2 0.0 copy-start.2
  94.2 5.5 %copy.14 = f32[32,256,128]{1,0,2:T(8,128)} copy(f32[32,256,128]{2,1,0:T(8,128)} %fusion.4) | data formatting | bytes 8388608 | tf_op jit(solution)/shard_map/sab,saf->sbf/dot_general | solution.py:10
  99.7 0.0 copy-done.2
  99.7 3.7 %fusion = f32[8,128,256]{2,0,1:T(8,128)S(1)} fusion(f32[32,256,128]{1,0,2:T(8,128)} %copy.14, s32[32]{0:T(128)S(1)} %bitcast.42, pred[32]{0:T(512)(128)(4,1)S(1)} %iota_compare_fusion.2), kind=kOutput, calls=%fused_computation.2 | convolution fusion | flops 100663808 | bytes 5243040 | tf_op jit(solution)/shard_map/sr,saf->raf/dot_general | solution.py:17
  103.4 1.3 copy.12
  104.7 0.0 reduce-scatter.5.cloned.1.call-update
  104.7 108.5 %all-reduce.2.cloned.1.call-done = f32[256,256]{1,0:T(8,128)} async-done(((f32[256,256]{1,0:T(8,128)}), f32[256,256]{1,0:T(8,128)}) %all-reduce.2.cloned.1.call-update) | async-done | bytes 262160 | tf_op jit(solution)/shard_map/psum | solution.py:21
  213.2 66.9 %reduce-scatter.5.cloned.1.call-done = f32[128,256]{1,0:T(8,128)} async-done(((f32[1024,256]{1,0:T(8,128)}), f32[128,256]{1,0:T(8,128)}) %reduce-scatter.5.cloned.1.call-update) | async-done | bytes 131088 | tf_op jit(solution)/shard_map/reduce_scatter | solution.py:65
  280.1 1.7 copy.17
  (4 shorter events, 0.0 us)
Async XLA Ops:
  7.2 36.7 %copy-start = (bf16[1,1,32,128,128]{4,3,2,1,0:T(8,128)(2,1)S(1)}, bf16[1,1,32,128,128]{4,3,2,1,0:T(8,128)(2,1)}, u32[]{:S(2)}) copy-start(bf16[1,1,32,128,128]{4,3,2,1,0:T(8,128)(2,1)} %param.9) | copy-start | bytes 3145732
  7.2 74.0 %reduce-scatter.3.cloned.1.call-start = ((), (), s32[]{:S(2)}) async-start(), calls=%async_computation.2 | async-start | bytes 655360 | tf_op jit(solution)/shard_map/reduce_scatter | solution.py:41
  48.1 5.5 %copy-start.1 = (s32[1,1,32]{2,1,0:T(1,128)S(1)}, s32[1,1,32]{2,1,0:T(1,128)}, u32[]{:S(2)}) copy-start(s32[1,1,32]{2,1,0:T(1,128)} %param.10) | copy-start | bytes 388
  53.6 27.5 %copy-start.3 = (bf16[256,256]{1,0:T(8,128)(2,1)S(1)}, bf16[256,256]{1,0:T(8,128)(2,1)}, u32[]{:S(2)}) copy-start(bf16[256,256]{1,0:T(8,128)(2,1)} %param.13) | copy-start | bytes 393220
  53.6 27.5 %copy-start.5 = (f32[256]{0:T(256)S(1)}, f32[256]{0:T(256)}, u32[]{:S(2)}) copy-start(f32[256]{0:T(256)} %param.14) | copy-start | bytes 3076
  57.3 25.6 %copy-start.4 = (bf16[128,256]{1,0:T(8,128)(2,1)S(1)}, bf16[128,256]{1,0:T(8,128)(2,1)}, u32[]{:S(2)}) copy-start(bf16[128,256]{1,0:T(8,128)(2,1)} %param.15) | copy-start | bytes 196612
  58.3 154.9 %all-reduce.2.cloned.1.call-start = ((), (), s32[]{:S(2)}) async-start(), calls=%async_computation.4 | async-start | bytes 524288 | tf_op jit(solution)/shard_map/psum | solution.py:21
  85.0 195.1 %reduce-scatter.5.cloned.1.call-start = ((), (), s32[]{:S(2)}) async-start(), calls=%async_computation.3 | async-start | bytes 1179648 | tf_op jit(solution)/shard_map/reduce_scatter | solution.py:65
  94.2 5.5 %copy-start.2 = (s32[1,1,32]{2,1,0:T(1,128)S(1)}, s32[1,1,32]{2,1,0:T(1,128)}, u32[]{:S(2)}) copy-start(s32[1,1,32]{2,1,0:T(1,128)} %param.11) | copy-start | bytes 388
Sparse Core Ops, SparseCore 0:
  58.4 22.7 reduce-scatter.2
  88.2 125.0 all-reduce.1
  217.6 62.5 reduce-scatter.4
where the time goes:
time: 289 us; the launch traced here: 288 us
  waiting for transfers between devices  198 us (69%)
  blocking collectives  39 us (13%)
  matrix products  18.1 us (6%)
  local copies, waits for them, and re-layouts  17.6 us (6%)
  between operations  14.5 us (5%)
    psum x1, waiting for transfers between devices, reduce_weight(): return lax.psum(local_weight, ('row', 'col'))  108 us
    reduce_scatter x1, waiting for transfers between devices, shards(): lax.psum_scatter(partial_grad.reshape(column_count * tile_size, feature_w...  66.9 us
    all_gather x1, blocking collectives, shards(): column_block = lax.all_gather(features, 'row', axis=0, tiled=True)  33.2 us
    reduce_scatter x1, waiting for transfers between devices, shards(): lax.psum_scatter(partial_value.reshape(row_count * tile_size, feature_wid...  22.8 us
    dot_general x2, matrix products, place(): jnp.einsum('sr,saf->raf', one_hot, products, precision=lax.Precision.HIGH...  7.38 us
    all_gather x1, blocking collectives, shards(): row_block = lax.all_gather(grad_aggregate, 'col', axis=0, tiled=True)  5.79 us
  transfers between devices with their start and end apart: 3, of which 3 were waited for; matrix products, arithmetic and copies ran while one was open for 5% of the time, Pallas kernels for 0%

commit v1 on v0

v1 whole, which is shorter than its diff:
```python
import functools

import jax
import jax.numpy as jnp
from jax import lax
from jax.experimental import pallas as pl
from jax.experimental.pallas import tpu as pltpu
from jax.sharding import PartitionSpec as P

F32 = jnp.float32
BF16 = jnp.bfloat16
GROUP = 16


def loop(count, body):
    if count <= 8:
        for step in range(count):
            body(step)
    else:
        lax.fori_loop(0, count, lambda step, carry: (body(step), carry)[1], 0)


def dot(a, b, dims=((1,), (0,))):
    return lax.dot_general(a, b, (dims, ((), ())), preferred_element_type=F32)


def kernel(
    n_row, n_col, fused_weight, pre_transpose,
    feat, tiles_hbm, row_ids, col_ids, live, weight, bias, cot,
    out, grad_feat, grad_w,
    tiles, adj, adj_t, gathered, acc, part_send, part_recv, grads, back_send, back_recv,
    w_local, w_col, w_piece, w_row, w_final, w_all,
    tile_sem, x_send, x_recv, p_send, p_recv, g_send, g_recv, b_send, b_recv,
    w1_send, w1_recv, w2_send, w2_recv, w3_send, w3_recv, w4_send, w4_recv,
):
    i = lax.axis_index("row")
    j = lax.axis_index("col")
    size = feat.shape[0]
    width = feat.shape[1]
    slots = tiles.shape[0]

    def row_peer(k):
        return lax.rem(i + k, n_row)

    def col_peer(k):
        return lax.rem(j + k, n_col)

    def send(src, dst, send_sem, recv_sem, axis, peer):
        return pltpu.make_async_remote_copy(
            src_ref=src, dst_ref=dst, send_sem=send_sem, recv_sem=recv_sem,
            device_id={axis: peer}, device_id_type=pl.DeviceIdType.MESH,
        )

    tile_copy = pltpu.make_async_copy(tiles_hbm.at[0, 0], tiles, tile_sem)
    tile_copy.start()

    barrier = pltpu.get_barrier_semaphore()

    def greet_row(k):
        pl.semaphore_signal(
            barrier, inc=1, device_id={"row": row_peer(k + 1)}, device_id_type=pl.DeviceIdType.MESH
        )

    def greet_col(k):
        pl.semaphore_signal(
            barrier, inc=1, device_id={"col": col_peer(k + 1)}, device_id_type=pl.DeviceIdType.MESH
        )

    loop(n_row - 1, greet_row)
    loop(n_col - 1, greet_col)
    pl.semaphore_wait(barrier, n_row + n_col - 2)

    def x_copy(to, sender):
        return send(feat, gathered.at[sender], x_send.at[to], x_recv.at[sender], "row", to)

    loop(n_row - 1, lambda k: x_copy(row_peer(k + 1), i).start())

    tile_copy.wait()
    depth = slots * GROUP
    together = n_row if n_row * n_col <= 64 else 1
    cells = together * n_col
    spread_in = (
        lax.broadcasted_iota(jnp.int32, (slots, depth), 1) // GROUP
        == lax.broadcasted_iota(jnp.int32, (slots, depth), 0)
    ).astype(BF16)
    spread_out = (
        lax.broadcasted_iota(jnp.int32, (cells * GROUP, cells), 0) // GROUP
        == lax.broadcasted_iota(jnp.int32, (cells * GROUP, cells), 1)
    ).astype(BF16)
    same_line = (
        lax.broadcasted_iota(jnp.int32, (cells * GROUP, depth), 0) % GROUP
        == lax.broadcasted_iota(jnp.int32, (cells * GROUP, depth), 1) % GROUP
    )
    cell_of = col_ids[0] * n_col + row_ids[0]
    cell_of = jnp.where(
        lax.broadcasted_iota(jnp.int32, (1, slots), 1) < live[...], cell_of, -1
    )

    def densify(step):
        cell_index = lax.broadcasted_iota(jnp.int32, (cells, slots), 0) + step * cells
        chosen = (cell_index == cell_of).astype(BF16)
        picked = dot(spread_out, dot(chosen, spread_in).astype(BF16))
        picked = jnp.where(same_line, picked, 0.0).astype(BF16)
        for pair in range(size // GROUP // 2):
            lines = [
                tiles[:, (2 * pair + h) * GROUP:(2 * pair + h + 1) * GROUP, :].reshape(depth, size)
                for h in range(2)
            ]
            block = dot(picked, jnp.concatenate(lines, axis=1)).astype(BF16)
            for c in range(together):
                for r in range(n_col):
                    at = (c * n_col + r) * GROUP
                    for h in range(2):
                        line = r * size + (2 * pair + h) * GROUP
                        adj[step * together + c, line:line + GROUP, :] = (
                            block[at:at + GROUP, h * size:(h + 1) * size]
                        )
        if pre_transpose:
            for c in range(together):
                adj_t[step * together + c] = adj[step * together + c].T

    loop(n_row // together, densify)

    rows = n_col * size
    chunk = min(rows, 512)

    def add_block(b, block, first):
        def one(step):
            at = pl.ds(step * chunk, chunk)
            product = dot(adj[b, at, :], block)
            if first:
                acc[at, :] = product
            else:
                acc[at, :] += product
        loop(rows // chunk, one)

    add_block(i, feat[...], True)

    def take_features(k):
        sender = lax.rem(i + n_row - 1 - k, n_row)
        x_copy(sender, sender).wait_recv()
        add_block(sender, gathered[sender], False)

    loop(n_row - 1, take_features)

    def p_copy(to, sender):
        return send(
            part_send.at[to], part_recv.at[sender], p_send.at[to], p_recv.at[sender], "col", to
        )

    def send_partial(k):
        to = col_peer(k + 1)
        part_send[to] = acc[pl.ds(pl.multiple_of(to * size, size), size), :].astype(BF16)
        p_copy(to, j).start()

    loop(n_col - 1, send_partial)
    acc_own = pl.ds(pl.multiple_of(j * size, size), size)

    def take_partial(k):
        sender = lax.rem(j + n_col - 1 - k, n_col)
        p_copy(sender, sender).wait_recv()
        acc[acc_own, :] += part_recv[sender].astype(F32)

    loop(n_col - 1, take_partial)

    aggregate = acc[acc_own, :].astype(BF16)
    preact = dot(aggregate, weight[...]) + bias[...]
    sig = jax.nn.sigmoid(preact)
    grad_pre = (cot[...].astype(F32) * sig * (1.0 + preact * (1.0 - sig))).astype(BF16)
    grads[j] = dot(grad_pre, weight[...], ((1,), (1,))).astype(BF16)

    def g_copy(to, sender):
        return send(grads.at[j], grads.at[sender], g_send.at[to], g_recv.at[sender], "col", to)

    loop(n_col - 1, lambda k: g_copy(col_peer(k + 1), j).start())

    out[...] = (preact * sig).astype(BF16)
    local_weight = dot(aggregate, grad_pre, ((0,), (0,)))

    if fused_weight:
        piece = width // n_col
        strip = piece // n_row
        w_local[...] = local_weight.reshape(n_col, piece, width).astype(BF16)

        def w1_copy(to, sender):
            return send(
                w_local.at[to], w_col.at[sender], w1_send.at[to], w1_recv.at[sender], "col", to
            )

        loop(n_col - 1, lambda k: w1_copy(col_peer(k + 1), j).start())
    else:
        grad_w[...] = local_weight

    def take_grad(k):
        sender = lax.rem(j + n_col - 1 - k, n_col)
        g_copy(sender, sender).wait_recv()

    loop(n_col - 1, take_grad)

    def back(b):
        if pre_transpose:
            return dot(adj_t[b], grads[...].reshape(rows, width))
        return dot(adj[b], grads[...].reshape(rows, width), ((0,), (0,)))

    def b_copy(to, sender):
        return send(
            back_send.at[to], back_recv.at[sender], b_send.at[to], b_recv.at[sender], "row", to
        )

    def send_back(k):
        to = row_peer(k + 1)
        back_send[to] = back(to).astype(BF16)
        b_copy(to, i).start()

    loop(n_row - 1, send_back)
    grad_feat[...] = back(i)

    if fused_weight:
        total = w_local[j].astype(F32)
        for k in range(n_col - 1):
            sender = lax.rem(j + n_col - 1 - k, n_col)
            w1_copy(sender, sender).wait_recv()
            total += w_col[sender].astype(F32)
        w_piece[...] = total.reshape(n_row, strip, width)

        def w2_copy(to, sender):
            return send(
                w_piece.at[to], w_row.at[sender], w2_send.at[to], w2_recv.at[sender], "row", to
            )

        loop(n_row - 1, lambda k: w2_copy(row_peer(k + 1), i).start())
        total = w_piece[i]
        for k in range(n_row - 1):
            sender = lax.rem(i + n_row - 1 - k, n_row)
            w2_copy(sender, sender).wait_recv()
            total += w_row[sender]
        w_final[i] = total

        def w3_copy(to, sender):
            return send(
                w_final.at[i], w_final.at[sender], w3_send.at[to], w3_recv.at[sender], "row", to
            )

        loop(n_row - 1, lambda k: w3_copy(row_peer(k + 1), i).start())
        for k in range(n_row - 1):
            sender = lax.rem(i + n_row - 1 - k, n_row)
            w3_copy(sender, sender).wait_recv()

        def w4_copy(to, sender):
            return send(
                w_final, w_all.at[sender], w4_send.at[to], w4_recv.at[sender], "col", to
            )

        loop(n_col - 1, lambda k: w4_copy(col_peer(k + 1), j).start())
        grad_w[j] = w_final[...].reshape(piece, width)

    def take_back(k):
        sender = lax.rem(i + n_row - 1 - k, n_row)
        b_copy(sender, sender).wait_recv()
        grad_feat[...] += back_recv[sender].astype(F32)

    loop(n_row - 1, take_back)

    if fused_weight:
        for k in range(n_col - 1):
            sender = lax.rem(j + n_col - 1 - k, n_col)
            w4_copy(sender, sender).wait_recv()
            grad_w[sender] = w_all[sender].reshape(piece, width)

    def row_sent(k):
        to = row_peer(k + 1)
        x_copy(to, i).wait_send()
        b_copy(to, i).wait_send()
        if fused_weight:
            w2_copy(to, i).wait_send()
            w3_copy(to, i).wait_send()

    def col_sent(k):
        to = col_peer(k + 1)
        p_copy(to, j).wait_send()
        g_copy(to, j).wait_send()
        if fused_weight:
            w1_copy(to, j).wait_send()
            w4_copy(to, j).wait_send()

    loop(n_row - 1, row_sent)
    loop(n_col - 1, col_sent)


def shards(n_row, n_col, features, tile_values, tile_rows, tile_cols, live_slots, weight, bias, cotangent):
    size, width = features.shape
    slots = tile_values.shape[2]
    out_width = weight.shape[1]
    rows = n_col * size
    fused_weight = width % (n_col * n_row * 8) == 0
    pre_transpose = n_row * n_col <= 64
    piece = width // n_col if fused_weight else 16
    strip = piece // n_row if fused_weight else 8
    w_shape = (n_col, piece, out_width) if fused_weight else (width, out_width)
    vmem = pl.BlockSpec(memory_space=pltpu.VMEM)
    row_dma = pltpu.SemaphoreType.DMA((n_row,))
    col_dma = pltpu.SemaphoreType.DMA((n_col,))
    out, grad_features, grad_weight = pl.pallas_call(
        functools.partial(kernel, n_row, n_col, fused_weight, pre_transpose),
        out_shape=(
            jax.ShapeDtypeStruct((size, out_width), BF16),
            jax.ShapeDtypeStruct((size, width), F32),
            jax.ShapeDtypeStruct(w_shape, F32),
        ),
        in_specs=[vmem, pl.BlockSpec(memory_space=pl.ANY)] + [vmem] * 6,
        out_specs=(vmem, vmem, vmem),
        scratch_shapes=[
            pltpu.VMEM((slots, size, size), BF16),
            pltpu.VMEM((n_row, rows, size), BF16),
            pltpu.VMEM((n_row, size, rows) if pre_transpose else (1, 16, 128), BF16),
            pltpu.VMEM((n_row, size, width), BF16),
            pltpu.VMEM((rows, width), F32),
            pltpu.VMEM((n_col, size, width), BF16),
            pltpu.VMEM((n_col, size, width), BF16),
            pltpu.VMEM((n_col, size, width), BF16),
            pltpu.VMEM((n_row, size, width), BF16),
            pltpu.VMEM((n_row, size, width), BF16),
            pltpu.VMEM((n_col, piece, out_width), BF16),
            pltpu.VMEM((n_col, piece, out_width), BF16),
            pltpu.VMEM((n_row, strip, out_width), F32),
            pltpu.VMEM((n_row, strip, out_width), F32),
            pltpu.VMEM((n_row, strip, out_width), F32),
            pltpu.VMEM((n_col, n_row, strip, out_width), F32),
            pltpu.SemaphoreType.DMA,
            row_dma, row_dma, col_dma, col_dma, col_dma, col_dma, row_dma, row_dma,
            col_dma, col_dma, row_dma, row_dma, row_dma, row_dma, col_dma, col_dma,
        ],
        compiler_params=pltpu.CompilerParams(
            collective_id=0, has_side_effects=True, vmem_limit_bytes=56 * 1024 * 1024
        ),
    )(
        features, tile_values, tile_rows, tile_cols, live_slots,
        weight, bias.reshape(1, out_width), cotangent,
    )
    if fused_weight:
        return out, grad_features, grad_weight.reshape(width, out_width)
    return out, grad_features, lax.psum(grad_weight, ("row", "col"))


def solution(mesh):
    return jax.shard_map(
        functools.partial(shards, mesh.shape["row"], mesh.shape["col"]),
        mesh=mesh,
        in_specs=(
            P(("col", "row"), None),
            P("row", "col", None, None, None),
            P("row", "col", None),
            P("row", "col", None),
            P("row", "col"),
            P(),
            P(),
            P(("row", "col"), None),
        ),
        out_specs=(P(("row", "col"), None), P(("col", "row"), None), P()),
        check_vma=False,
    )
```

time: 289 us -> 58.3 us (0.20)
  waiting for transfers between devices: 198 us -> 0 us
  Pallas kernels: 0 us -> 53 us
  blocking collectives: 39 us -> 0 us
  matrix products: 18.1 us -> 0 us
  local copies, waits for them, and re-layouts: 17.6 us -> 3.79 us
  between operations: 14.5 us -> 1.3 us
    psum x1 -> x0, waiting for transfers between devices: 108 us -> none  [reduce_weight(): return lax.psum(local_weight, ('row', 'col'))]
    reduce_scatter x2 -> x0, waiting for transfers between devices: 89.8 us -> none  [the longest x1 66.9 us: shards(): lax.psum_scatter(partial_grad.reshape(column_count * tile_size, feature_w...]
    pallas_call x0 -> x1, Pallas kernels: none -> 53 us  [shards(): pl.pallas_call(functools.partial(kernel, n_row, n_col, fused_weight, pre_...]
    all_gather x2 -> x0, blocking collectives: 39 us -> none  [the longest x1 33.2 us: shards(): column_block = lax.all_gather(features, 'row', axis=0, tiled=True)]
    dot_general x7 -> x0, matrix products: 18.1 us -> none  [the longest x2 7.38 us: place(): jnp.einsum('sr,saf->raf', one_hot, products, precision=lax.Precision.HIGH...]
    dot_general x4 -> x0, local copies, waits for them, and re-layouts: 13.2 us -> none  [the longest x1 5.5 us: tile_products(): jnp.einsum('sab,saf->sbf', tiles, picked, preferred_element_type=jnp.floa...]
  transfers between devices with their start and end apart: 3 -> 0, of which waited for: 3 -> 0; matrix products, arithmetic and copies ran while one was open for 5% -> 0% of each run, Pallas kernels for 0% -> 0%
where the time goes in v1:
time: 58.3 us; the launch traced here: 58 us
  Pallas kernels  53 us (91%)
  local copies, waits for them, and re-layouts  3.79 us (7%)
  between operations  1.3 us (2%)
    pallas_call x1, Pallas kernels, shards(): pl.pallas_call(functools.partial(kernel, n_row, n_col, fused_weight, pre_...  53 us
    unnamed x5, local copies, waits for them, and re-layouts  3.79 us

profile of v1, /device:TPU:0, one launch (start us, length us, event | category | flops | bytes accessed | tf_op | source)
XLA Modules:
  0.0 58.0 jit_solution(3202297764823202625)
XLA Ops:
  1.3 53.0 %shard_map.103 = (bf16[128,256]{1,0:T(8,128)(2,1)}, f32[128,256]{1,0:T(8,128)}, f32[4,64,256]{2,1,0:T(8,128)}) custom-call(bf16[128,256]{1,0:T(8,128)(2,1)} %feat.1, bf16[1,1,32,128,128]{4,3,2,1,0:T(8,128)(2,1)} %tiles_hbm.1, s32[1,1,32]{2,1,0:T(1,128)} %row_ids.1, s32[1,1,32]{2,1,0:T(1,128)} %col_ids.1, s32[1,1]{1,0:T(1,128)S(6)} %copy.14.live, ...), custom_call_target="tpu_custom_call" | custom-call | tf_op jit(solution)/shard_map/pallas_call | solution.py:303
  54.2 0.0 copy-start
  54.3 1.5 %copy.15 = bf16[128,256]{1,0:T(8,128)(2,1)} copy(bf16[128,256]{1,0:T(8,128)(2,1)} %get-tuple-element.12) | data formatting | bytes 131072
  55.8 1.6 %copy.16 = f32[128,256]{1,0:T(8,128)} copy(f32[128,256]{1,0:T(8,128)} %get-tuple-element.13) | data formatting | bytes 262144
  57.3 0.0 copy-done
  57.3 0.7 %copy.17 = f32[256,256]{1,0:T(8,128)} copy(f32[256,256]{1,0:T(8,128)S(1)} %bitcast.2) | data formatting | bytes 524288
Async XLA Ops:
  54.2 3.1 %copy-start = (f32[4,64,256]{2,1,0:T(8,128)S(1)}, f32[4,64,256]{2,1,0:T(8,128)}, u32[]{:S(2)}) copy-start(f32[4,64,256]{2,1,0:T(8,128)} %get-tuple-element.8) | copy-start | bytes 786436

commit v2 on v1

v2 whole, which is shorter than its diff:
```python
import functools

import jax
import jax.numpy as jnp
from jax import lax
from jax.experimental import pallas as pl
from jax.experimental.pallas import tpu as pltpu
from jax.sharding import PartitionSpec as P

F32 = jnp.float32
BF16 = jnp.bfloat16
GROUP = 16


def loop(count, body):
    if count <= 8:
        for step in range(count):
            body(step)
    else:
        lax.fori_loop(0, count, lambda step, carry: (body(step), carry)[1], 0)


def dot(a, b, dims=((1,), (0,))):
    return lax.dot_general(a, b, (dims, ((), ())), preferred_element_type=F32)


def kernel(
    n_row, n_col, outer, pre_transpose,
    feat, tiles_hbm, row_ids, col_ids, live, weight, bias, cot,
    out, grad_feat, grad_w,
    tiles, adj, adj_t, gathered, acc, part_send, part_recv, grads,
    y_out, y_in, keep, z_out, z_in, w_out, w_in, w_sum, w_cols, w_all,
    tile_sem, xz_send, xy_send, x_recv, p_send, p_recv, g_send, g_recv,
    by_send, by_recv, bz_send, bz_recv,
    w1_send, w1_recv, w2_send, w2_recv, w3z_send, w3y_send, w3_recv,
):
    i = lax.axis_index("row")
    j = lax.axis_index("col")
    inner = n_row // outer
    z = i // inner
    y = i % inner
    size = feat.shape[0]
    slots = tiles.shape[0]

    def row_peer(k):
        return lax.rem(i + k, n_row)

    def col_peer(k):
        return lax.rem(j + k, n_col)

    def y_peer(k):
        return lax.rem(y + k, inner)

    if outer == 4:
        near, mid, far = z + 1 - 2 * (z % 2), (z + 2) % 4, 3 - z
        z_near_first, z_far_first = (near, mid, far), (mid, far, near)
    else:
        z_near_first = z_far_first = tuple((z + k) % outer for k in range(1, outer))

    def send(src, dst, send_sem, recv_sem, axis, peer):
        return pltpu.make_async_remote_copy(
            src_ref=src, dst_ref=dst, send_sem=send_sem, recv_sem=recv_sem,
            device_id={axis: peer}, device_id_type=pl.DeviceIdType.MESH,
        )

    tile_copy = pltpu.make_async_copy(tiles_hbm.at[0, 0], tiles, tile_sem)
    tile_copy.start()

    barrier = pltpu.get_barrier_semaphore()

    def greet_row(k):
        pl.semaphore_signal(
            barrier, inc=1, device_id={"row": row_peer(k + 1)}, device_id_type=pl.DeviceIdType.MESH
        )

    def greet_col(k):
        pl.semaphore_signal(
            barrier, inc=1, device_id={"col": col_peer(k + 1)}, device_id_type=pl.DeviceIdType.MESH
        )

    loop(n_row - 1, greet_row)
    loop(n_col - 1, greet_col)
    gathered[i] = feat[...]
    pl.semaphore_wait(barrier, n_row + n_col - 2)

    def along_z(buf, z_sem, recv_sem, to, block):
        return send(
            buf.at[block], buf.at[block], z_sem.at[to], recv_sem.at[block], "row", to * inner + y
        )

    def along_y(buf, y_sem, recv_sem, block_z, to, block):
        return send(
            buf.at[block], buf.at[block], y_sem.at[block_z * inner + to], recv_sem.at[block],
            "row", z * inner + to,
        )

    def gather_start(buf, z_sem, y_sem, recv_sem):
        for to in z_far_first:
            along_z(buf, z_sem, recv_sem, to, i).start()
        loop(inner - 1, lambda k: along_y(buf, y_sem, recv_sem, z, y_peer(k + 1), i).start())

    def gather_pass(buf, z_sem, y_sem, recv_sem, block_z):
        block = block_z * inner + y
        along_z(buf, z_sem, recv_sem, block_z, block).wait_recv()
        loop(
            inner - 1,
            lambda k: along_y(buf, y_sem, recv_sem, block_z, y_peer(k + 1), block).start(),
        )
        return block

    def gather_take(buf, y_sem, recv_sem, block_z, from_y):
        block = block_z * inner + from_y
        along_y(buf, y_sem, recv_sem, block_z, from_y, block).wait_recv()
        return block

    def gather_sent(buf, z_sem, y_sem, recv_sem):
        for to in z_near_first:
            along_z(buf, z_sem, recv_sem, to, i).wait_send()
        for block_z in (z,) + z_near_first:
            loop(
                inner - 1,
                lambda k: along_y(
                    buf, y_sem, recv_sem, block_z, y_peer(k + 1), block_z * inner + y
                ).wait_send(),
            )

    x_refs = (gathered, xz_send, xy_send, x_recv)
    gather_start(*x_refs)

    tile_copy.wait()
    depth = slots * GROUP
    together = n_row if n_row * n_col <= 64 else 1
    cells = together * n_col
    spread_in = (
        lax.broadcasted_iota(jnp.int32, (slots, depth), 1) // GROUP
        == lax.broadcasted_iota(jnp.int32, (slots, depth), 0)
    ).astype(BF16)
    spread_out = (
        lax.broadcasted_iota(jnp.int32, (cells * GROUP, cells), 0) // GROUP
        == lax.broadcasted_iota(jnp.int32, (cells * GROUP, cells), 1)
    ).astype(BF16)
    same_line = (
        lax.broadcasted_iota(jnp.int32, (cells * GROUP, depth), 0) % GROUP
        == lax.broadcasted_iota(jnp.int32, (cells * GROUP, depth), 1) % GROUP
    )
    cell_of = col_ids[0] * n_col + row_ids[0]
    cell_of = jnp.where(
        lax.broadcasted_iota(jnp.int32, (1, slots), 1) < live[...], cell_of, -1
    )

    def densify(step):
        cell_index = lax.broadcasted_iota(jnp.int32, (cells, slots), 0) + step * cells
        chosen = (cell_index == cell_of).astype(BF16)
        picked = dot(spread_out, dot(chosen, spread_in).astype(BF16))
        picked = jnp.where(same_line, picked, 0.0).astype(BF16)
        for pair in range(size // GROUP // 2):
            lines = [
                tiles[:, (2 * pair + h) * GROUP:(2 * pair + h + 1) * GROUP, :].reshape(depth, size)
                for h in range(2)
            ]
            block = dot(picked, jnp.concatenate(lines, axis=1)).astype(BF16)
            for c in range(together):
                for r in range(n_col):
                    at = (c * n_col + r) * GROUP
                    for h in range(2):
                        line = r * size + (2 * pair + h) * GROUP
                        adj[step * together + c, line:line + GROUP, :] = (
                            block[at:at + GROUP, h * size:(h + 1) * size]
                        )
        if pre_transpose:
            for c in range(together):
                adj_t[step * together + c] = adj[step * together + c].T

    loop(n_row // together, densify)

    rows = n_col * size
    chunk = min(rows, 512)

    def add_block(b, block, first):
        def one(step):
            at = pl.ds(step * chunk, chunk)
            product = dot(adj[b, at, :], block)
            if first:
                acc[at, :] = product
            else:
                acc[at, :] += product
        loop(rows // chunk, one)

    add_block(i, feat[...], True)
    for block_z in z_near_first:
        block = gather_pass(*x_refs, block_z)
        add_block(block, gathered[block], False)
    for block_z in (z,) + z_near_first:
        def take_features(k):
            block = gather_take(gathered, xy_send, x_recv, block_z, y_peer(k + 1))
            add_block(block, gathered[block], False)
        loop(inner - 1, take_features)

    def p_copy(to, sender):
        return send(
            part_send.at[to], part_recv.at[sender], p_send.at[to], p_recv.at[sender], "col", to
        )

    def send_partial(k):
        to = col_peer(k + 1)
        part_send[to] = acc[pl.ds(pl.multiple_of(to * size, size), size), :].astype(BF16)
        p_copy(to, j).start()

    loop(n_col - 1, send_partial)
    acc_own = pl.ds(pl.multiple_of(j * size, size), size)

    def take_partial(k):
        sender = lax.rem(j + n_col - 1 - k, n_col)
        p_copy(sender, sender).wait_recv()
        acc[acc_own, :] += part_recv[sender].astype(F32)

    loop(n_col - 1, take_partial)

    aggregate = acc[acc_own, :].astype(BF16)
    preact = dot(aggregate, weight[...]) + bias[...]
    sig = jax.nn.sigmoid(preact)
    grad_pre = (cot[...].astype(F32) * sig * (1.0 + preact * (1.0 - sig))).astype(BF16)
    grads[j] = dot(grad_pre, weight[...], ((1,), (1,))).astype(BF16)

    def g_copy(to, sender):
        return send(grads.at[j], grads.at[sender], g_send.at[to], g_recv.at[sender], "col", to)

    loop(n_col - 1, lambda k: g_copy(col_peer(k + 1), j).start())

    out[...] = (preact * sig).astype(BF16)
    local_weight = dot(aggregate, grad_pre, ((0,), (0,)))


    w_out[...] = local_weight.reshape(w_out.shape).astype(w_out.dtype)

    def w1_copy(to, sender):
        return send(w_out.at[to], w_in.at[sender], w1_send.at[to], w1_recv.at[sender], "row", to)

    loop(n_row - 1, lambda k: w1_copy(row_peer(k + 1), i).start())

    def take_grad(k):
        sender = lax.rem(j + n_col - 1 - k, n_col)
        g_copy(sender, sender).wait_recv()

    loop(n_col - 1, take_grad)

    def back(b):
        grad_rows = grads[...].reshape(rows, grads.shape[2])
        if pre_transpose:
            return dot(adj_t[b], grad_rows)
        return dot(adj[b], grad_rows, ((0,), (0,)))

    def by_copy(block_z, to, sender):
        return send(
            y_out.at[block_z * inner + to], y_in.at[block_z * inner + sender],
            by_send.at[block_z * inner + to], by_recv.at[block_z * inner + sender],
            "row", z * inner + to,
        )

    def bz_copy(to, sender):
        return send(
            z_out.at[to], z_in.at[sender], bz_send.at[to], bz_recv.at[sender],
            "row", to * inner + y,
        )

    for block_z in z_far_first + (z,):
        def send_back(k):
            to = y_peer(k + 1)
            y_out[block_z * inner + to] = back(block_z * inner + to).astype(BF16)
            by_copy(block_z, to, y).start()
        loop(inner - 1, send_back)
    for block_z in z_far_first + (z,):
        keep[block_z] = back(block_z * inner + y)

    w_sum[...] = w_out[i].astype(F32)

    def take_w1(k):
        sender = lax.rem(i + n_row - 1 - k, n_row)
        w1_copy(sender, sender).wait_recv()
        w_sum[...] += w_in[sender].astype(F32)

    loop(n_row - 1, take_w1)

    def w2_copy(to, sender):
        return send(w_sum, w_cols.at[sender], w2_send.at[to], w2_recv.at[sender], "col", to)

    loop(n_col - 1, lambda k: w2_copy(col_peer(k + 1), j).start())

    def add_back(block_z):
        def take(k):
            sender = lax.rem(y + inner - 1 - k, inner)
            by_copy(block_z, sender, sender).wait_recv()
            keep[block_z] += y_in[block_z * inner + sender].astype(F32)
        loop(inner - 1, take)

    for block_z in z_far_first:
        add_back(block_z)
        z_out[block_z] = keep[block_z].astype(BF16)
        bz_copy(block_z, z).start()

    w_cols[j] = w_sum[...]

    def take_w2(k):
        sender = lax.rem(j + n_col - 1 - k, n_col)
        w2_copy(sender, sender).wait_recv()

    loop(n_col - 1, take_w2)
    w_all[i] = jnp.sum(w_cols[...], axis=0).astype(w_all.dtype)
    w_refs = (w_all, w3z_send, w3y_send, w3_recv)
    gather_start(*w_refs)

    add_back(z)
    for block_z in z_near_first:
        gather_pass(*w_refs, block_z)
    total = keep[z]
    for block_z in z_near_first:
        bz_copy(block_z, block_z).wait_recv()
        total += z_in[block_z].astype(F32)
    grad_feat[...] = total
    for block_z in (z,) + z_near_first:
        loop(
            inner - 1,
            lambda k: gather_take(w_all, w3y_send, w3_recv, block_z, y_peer(k + 1)),
        )
    grad_w[...] = w_all[...].reshape(grad_w.shape).astype(F32)

    gather_sent(*x_refs)
    gather_sent(*w_refs)
    loop(n_row - 1, lambda k: w1_copy(row_peer(k + 1), i).wait_send())

    def col_sent(k):
        to = col_peer(k + 1)
        p_copy(to, j).wait_send()
        g_copy(to, j).wait_send()
        w2_copy(to, j).wait_send()

    loop(n_col - 1, col_sent)
    for block_z in z_near_first:
        bz_copy(block_z, z).wait_send()
    for block_z in (z,) + z_near_first:
        loop(inner - 1, lambda k: by_copy(block_z, y_peer(k + 1), y).wait_send())


def shards(n_row, n_col, features, tile_values, tile_rows, tile_cols, live_slots, weight, bias, cotangent):
    size, width = features.shape
    slots = tile_values.shape[2]
    out_width = weight.shape[1]
    rows = n_col * size
    outer = 4 if n_row % 4 == 0 else 1
    inner = n_row // outer
    pre_transpose = n_row * n_col <= 64
    strip = width // n_row
    w_kind = BF16 if strip % 16 == 0 else F32
    vmem = pl.BlockSpec(memory_space=pltpu.VMEM)
    anywhere = pl.BlockSpec(memory_space=pl.ANY)
    row_dma = pltpu.SemaphoreType.DMA((n_row,))
    col_dma = pltpu.SemaphoreType.DMA((n_col,))
    z_dma = pltpu.SemaphoreType.DMA((outer,))
    out_shape = (
        jax.ShapeDtypeStruct((size, out_width), BF16),
        jax.ShapeDtypeStruct((size, width), F32),
        jax.ShapeDtypeStruct((width, out_width), F32),
    )
    results = pl.pallas_call(
        functools.partial(kernel, n_row, n_col, outer, pre_transpose),
        out_shape=out_shape,
        in_specs=[vmem, anywhere] + [vmem] * 6,
        out_specs=(vmem, vmem, vmem),
        scratch_shapes=[
            pltpu.VMEM((slots, size, size), BF16),
            pltpu.VMEM((n_row, rows, size), BF16),
            pltpu.VMEM((n_row, size, rows) if pre_transpose else (1, 16, 128), BF16),
            pltpu.VMEM((n_row, size, width), BF16),
            pltpu.VMEM((rows, width), F32),
            pltpu.VMEM((n_col, size, width), BF16),
            pltpu.VMEM((n_col, size, width), BF16),
            pltpu.VMEM((n_col, size, width), BF16),
            pltpu.VMEM((n_row, size, width), BF16),
            pltpu.VMEM((n_row, size, width), BF16),
            pltpu.VMEM((outer, size, width), F32),
            pltpu.VMEM((outer, size, width), BF16),
            pltpu.VMEM((outer, size, width), BF16),
            pltpu.VMEM((n_row, strip, out_width), w_kind),
            pltpu.VMEM((n_row, strip, out_width), w_kind),
            pltpu.VMEM((strip, out_width), F32),
            pltpu.VMEM((n_col, strip, out_width), F32),
            pltpu.VMEM((n_row, strip, out_width), w_kind),
            pltpu.SemaphoreType.DMA,
            z_dma, row_dma, row_dma, col_dma, col_dma, col_dma, col_dma,
            row_dma, row_dma, z_dma, z_dma,
            row_dma, row_dma, col_dma, col_dma, z_dma, row_dma, row_dma,
        ],
        compiler_params=pltpu.CompilerParams(
            collective_id=0, has_side_effects=True, vmem_limit_bytes=56 * 1024 * 1024
        ),
    )(
        features, tile_values, tile_rows, tile_cols, live_slots,
        weight, bias.reshape(1, out_width), cotangent,
    )
    return results


def solution(mesh):
    return jax.shard_map(
        functools.partial(shards, mesh.shape["row"], mesh.shape["col"]),
        mesh=mesh,
        in_specs=(
            P(("col", "row"), None),
            P("row", "col", None, None, None),
            P("row", "col", None),
            P("row", "col", None),
            P("row", "col"),
            P(),
            P(),
            P(("row", "col"), None),
        ),
        out_specs=(P(("row", "col"), None), P(("col", "row"), None), P()),
        check_vma=False,
    )
```

time: 58.3 us -> 48.5 us (0.83)
  Pallas kernels: 53 us -> 43.2 us
    pallas_call x1, Pallas kernels: 53 us -> 43.2 us  [shards(): pl.pallas_call(functools.partial(kernel, n_row, n_col, outer, pre_transpo...]
where the time goes in v2:
time: 48.5 us; the launch traced here: 48.3 us
  Pallas kernels  43.2 us (89%)
  local copies, waits for them, and re-layouts  3.79 us (8%)
  between operations  1.3 us (3%)
    pallas_call x1, Pallas kernels, shards(): pl.pallas_call(functools.partial(kernel, n_row, n_col, outer, pre_transpo...  43.2 us
    unnamed x5, local copies, waits for them, and re-layouts  3.79 us

profile of v2, /device:TPU:0, one launch (start us, length us, event | category | flops | bytes accessed | tf_op | source)
XLA Modules:
  0.0 48.3 jit_solution(1283582772391005270)
XLA Ops:
  1.3 43.2 %shard_map.103 = (bf16[128,256]{1,0:T(8,128)(2,1)}, f32[128,256]{1,0:T(8,128)}, f32[256,256]{1,0:T(8,128)}) custom-call(bf16[128,256]{1,0:T(8,128)(2,1)} %feat.1, bf16[1,1,32,128,128]{4,3,2,1,0:T(8,128)(2,1)} %tiles_hbm.1, s32[1,1,32]{2,1,0:T(1,128)} %row_ids.1, s32[1,1,32]{2,1,0:T(1,128)} %col_ids.1, s32[1,1]{1,0:T(1,128)S(6)} %copy.14.live, ...), custom_call_target="tpu_custom_call" | custom-call | tf_op jit(solution)/shard_map/pallas_call | solution.py:364
  44.5 0.0 copy-start
  44.5 1.5 %copy.15 = bf16[128,256]{1,0:T(8,128)(2,1)} copy(bf16[128,256]{1,0:T(8,128)(2,1)} %get-tuple-element.6) | data formatting | bytes 131072
  46.0 1.6 %copy.16 = f32[128,256]{1,0:T(8,128)} copy(f32[128,256]{1,0:T(8,128)} %get-tuple-element.7) | data formatting | bytes 262144
  47.6 0.0 copy-done
  47.6 0.7 %copy.17 = f32[256,256]{1,0:T(8,128)} copy(f32[256,256]{1,0:T(8,128)S(1)} %copy-done) | data formatting | bytes 524288
Async XLA Ops:
  44.5 3.1 %copy-start = (f32[256,256]{1,0:T(8,128)S(1)}, f32[256,256]{1,0:T(8,128)}, u32[]{:S(2)}) copy-start(f32[256,256]{1,0:T(8,128)} %get-tuple-element.8) | copy-start | bytes 786436

commit v3 on v2

--- a/solution.py
+++ b/solution.py
@@ -26,13 +26,14 @@
 
 def kernel(
     n_row, n_col, outer, pre_transpose,
-    feat, tiles_hbm, row_ids, col_ids, live, weight, bias, cot,
-    out, grad_feat, grad_w,
+    feat_hbm, tiles_hbm, row_ids_hbm, col_ids_hbm, live, weight_hbm, bias_hbm, cot_hbm,
+    out_hbm, grad_feat_hbm, grad_w_hbm,
+    feat, row_ids, col_ids, weight, bias, cot, out, grad_feat, grad_w,
     tiles, adj, adj_t, gathered, acc, part_send, part_recv, grads,
     y_out, y_in, keep, z_out, z_in, w_out, w_in, w_sum, w_cols, w_all,
-    tile_sem, xz_send, xy_send, x_recv, p_send, p_recv, g_send, g_recv,
+    load_sems, store_sems, tile_sem, xz_send, xy_send, x_recv, p_send, p_recv, g_send, g_recv,
     by_send, by_recv, bz_send, bz_recv,
-    w1_send, w1_recv, w2_send, w2_recv, w3z_send, w3y_send, w3_recv,
+    w1_send, w1_recv, w2_send, w2_recv, w3_send, w3_recv,
 ):
     i = lax.axis_index("row")
     j = lax.axis_index("col")
@@ -53,7 +54,9 @@
 
     if outer == 4:
         near, mid, far = z + 1 - 2 * (z % 2), (z + 2) % 4, 3 - z
-        z_near_first, z_far_first = (near, mid, far), (mid, far, near)
+        within = (z % 3 + 1) // 2
+        z_near_first = (near, mid + within * (far - mid), far + within * (mid - far))
+        z_far_first = (mid, far, near)
     else:
         z_near_first = z_far_first = tuple((z + k) % outer for k in range(1, outer))
 
@@ -63,8 +66,24 @@
             device_id={axis: peer}, device_id_type=pl.DeviceIdType.MESH,
         )
 
+    loads = [
+        pltpu.make_async_copy(src, dst, load_sems.at[k])
+        for k, (src, dst) in enumerate((
+            (feat_hbm, feat), (row_ids_hbm, row_ids), (col_ids_hbm, col_ids),
+            (weight_hbm, weight), (bias_hbm, bias), (cot_hbm, cot),
+        ))
+    ]
+    stores = [
+        pltpu.make_async_copy(src, dst, store_sems.at[k])
+        for k, (src, dst) in enumerate((
+            (out, out_hbm), (grad_feat, grad_feat_hbm), (grad_w, grad_w_hbm),
+        ))
+    ]
     tile_copy = pltpu.make_async_copy(tiles_hbm.at[0, 0], tiles, tile_sem)
+    loads[0].start()
     tile_copy.start()
+    for load in loads[1:]:
+        load.start()
 
     barrier = pltpu.get_barrier_semaphore()
 
@@ -80,6 +99,7 @@
 
     loop(n_row - 1, greet_row)
     loop(n_col - 1, greet_col)
+    loads[0].wait()
     gathered[i] = feat[...]
     pl.semaphore_wait(barrier, n_row + n_col - 2)
 
@@ -95,7 +115,7 @@
         )
 
     def gather_start(buf, z_sem, y_sem, recv_sem):
-        for to in z_far_first:
+        for to in z_near_first:
             along_z(buf, z_sem, recv_sem, to, i).start()
         loop(inner - 1, lambda k: along_y(buf, y_sem, recv_sem, z, y_peer(k + 1), i).start())
 
@@ -128,6 +148,8 @@
     gather_start(*x_refs)
 
     tile_copy.wait()
+    loads[1].wait()
+    loads[2].wait()
     depth = slots * GROUP
     together = n_row if n_row * n_col <= 64 else 1
     cells = together * n_col
@@ -217,6 +239,8 @@
     loop(n_col - 1, take_partial)
 
     aggregate = acc[acc_own, :].astype(BF16)
+    for load in loads[3:]:
+        load.wait()
     preact = dot(aggregate, weight[...]) + bias[...]
     sig = jax.nn.sigmoid(preact)
     grad_pre = (cot[...].astype(F32) * sig * (1.0 + preact * (1.0 - sig))).astype(BF16)
@@ -228,6 +252,7 @@
     loop(n_col - 1, lambda k: g_copy(col_peer(k + 1), j).start())
 
     out[...] = (preact * sig).astype(BF16)
+    stores[0].start()
     local_weight = dot(aggregate, grad_pre, ((0,), (0,)))
 
 
@@ -293,11 +318,14 @@
             keep[block_z] += y_in[block_z * inner + sender].astype(F32)
         loop(inner - 1, take)
 
-    for block_z in z_far_first:
+    def pass_back(block_z):
         add_back(block_z)
         z_out[block_z] = keep[block_z].astype(BF16)
         bz_copy(block_z, z).start()
 
+    for block_z in z_far_first[:2]:
+        pass_back(block_z)
+
     w_cols[j] = w_sum[...]
 
     def take_w2(k):
@@ -306,27 +334,35 @@
 
     loop(n_col - 1, take_w2)
     w_all[i] = jnp.sum(w_cols[...], axis=0).astype(w_all.dtype)
-    w_refs = (w_all, w3z_send, w3y_send, w3_recv)
-    gather_start(*w_refs)
-
+
+    def w3_copy(to, sender):
+        return send(
+            w_all.at[sender], w_all.at[sender], w3_send.at[to], w3_recv.at[sender], "row", to
+        )
+
+    loop(n_row - 1, lambda k: w3_copy(row_peer(k + 1), i).start())
+
+    for block_z in z_far_first[2:]:
+        pass_back(block_z)
     add_back(z)
-    for block_z in z_near_first:
-        gather_pass(*w_refs, block_z)
     total = keep[z]
     for block_z in z_near_first:
         bz_copy(block_z, block_z).wait_recv()
         total += z_in[block_z].astype(F32)
     grad_feat[...] = total
-    for block_z in (z,) + z_near_first:
-        loop(
-            inner - 1,
-            lambda k: gather_take(w_all, w3y_send, w3_recv, block_z, y_peer(k + 1)),
-        )
+    stores[1].start()
+
+    def take_w3(k):
+        sender = lax.rem(i + n_row - 1 - k, n_row)
+        w3_copy(sender, sender).wait_recv()
+
+    loop(n_row - 1, take_w3)
     grad_w[...] = w_all[...].reshape(grad_w.shape).astype(F32)
+    stores[2].start()
 
     gather_sent(*x_refs)
-    gather_sent(*w_refs)
     loop(n_row - 1, lambda k: w1_copy(row_peer(k + 1), i).wait_send())
+    loop(n_row - 1, lambda k: w3_copy(row_peer(k + 1), i).wait_send())
 
     def col_sent(k):
         to = col_peer(k + 1)
@@ -339,6 +375,22 @@
         bz_copy(block_z, z).wait_send()
     for block_z in (z,) + z_near_first:
         loop(inner - 1, lambda k: by_copy(block_z, y_peer(k + 1), y).wait_send())
+    for store in stores:
+        store.wait()
+
+
+def hand_over(*refs):
+    sources, results, held = refs[:3], refs[3:6], refs[6:9]
+    sems = refs[9]
+    loads = [pltpu.make_async_copy(sources[k], held[k], sems.at[k]) for k in range(3)]
+    stores = [pltpu.make_async_copy(held[k], results[k], sems.at[3 + k]) for k in range(3)]
+    for load in loads:
+        load.start()
+    for load, store in zip(loads, stores):
+        load.wait()
+        store.start()
+    for store in stores:
+        store.wait()
 
 
 def shards(n_row, n_col, features, tile_values, tile_rows, tile_cols, live_slots, weight, bias, cotangent):
@@ -364,9 +416,18 @@
     results = pl.pallas_call(
         functools.partial(kernel, n_row, n_col, outer, pre_transpose),
         out_shape=out_shape,
-        in_specs=[vmem, anywhere] + [vmem] * 6,
-        out_specs=(vmem, vmem, vmem),
+        in_specs=[anywhere] * 4 + [vmem] + [anywhere] * 3,
+        out_specs=(anywhere,) * 3,
         scratch_shapes=[
+            pltpu.VMEM((size, width), BF16),
+            pltpu.VMEM((1, 1, slots), jnp.int32),
+            pltpu.VMEM((1, 1, slots), jnp.int32),
+            pltpu.VMEM((width, out_width), BF16),
+            pltpu.VMEM((1, out_width), F32),
+            pltpu.VMEM((size, out_width), BF16),
+            pltpu.VMEM((size, out_width), BF16),
+            pltpu.VMEM((size, width), F32),
+            pltpu.VMEM((width, out_width), F32),
             pltpu.VMEM((slots, size, size), BF16),
             pltpu.VMEM((n_row, rows, size), BF16),
             pltpu.VMEM((n_row, size, rows) if pre_transpose else (1, 16, 128), BF16),
@@ -385,10 +446,12 @@
             pltpu.VMEM((strip, out_width), F32),
             pltpu.VMEM((n_col, strip, out_width), F32),
             pltpu.VMEM((n_row, strip, out_width), w_kind),
+            pltpu.SemaphoreType.DMA((6,)),
+            pltpu.SemaphoreType.DMA((3,)),
             pltpu.SemaphoreType.DMA,
             z_dma, row_dma, row_dma, col_dma, col_dma, col_dma, col_dma,
             row_dma, row_dma, z_dma, z_dma,
-            row_dma, row_dma, col_dma, col_dma, z_dma, row_dma, row_dma,
+            row_dma, row_dma, col_dma, col_dma, row_dma, row_dma,
         ],
         compiler_params=pltpu.CompilerParams(
             collective_id=0, has_side_effects=True, vmem_limit_bytes=56 * 1024 * 1024
@@ -397,7 +460,14 @@
         features, tile_values, tile_rows, tile_cols, live_slots,
         weight, bias.reshape(1, out_width), cotangent,
     )
-    return results
+    return pl.pallas_call(
+        hand_over,
+        out_shape=out_shape,
+        in_specs=[anywhere] * 3,
+        out_specs=(anywhere,) * 3,
+        scratch_shapes=[pltpu.VMEM(a.shape, a.dtype) for a in out_shape]
+        + [pltpu.SemaphoreType.DMA((6,))],
+    )(*results)
 
 
 def solution(mesh):

time: 48.5 us -> 42.5 us (0.88)
  local copies, waits for them, and re-layouts: 3.79 us -> 0 us
  Pallas kernels: 43.2 us -> 41.1 us
    pallas_call x1, Pallas kernels: 43.2 us -> 39.3 us  [shards(): pl.pallas_call(functools.partial(kernel, n_row, n_col, outer, pre_transpo...]
    unnamed x5 -> x0, local copies, waits for them, and re-layouts: 3.79 us -> none
    pallas_call x0 -> x1, Pallas kernels: none -> 1.81 us  [shards(): pl.pallas_call(hand_over, out_shape=out_shape, in_specs=[anywhere] * 3, o...]
where the time goes in v3:
time: 42.5 us; the launch traced here: 42.4 us
  Pallas kernels  41.1 us (97%)
  between operations  1.29 us (3%)
    pallas_call x1, Pallas kernels, shards(): pl.pallas_call(functools.partial(kernel, n_row, n_col, outer, pre_transpo...  39.3 us
    pallas_call x1, Pallas kernels, shards(): pl.pallas_call(hand_over, out_shape=out_shape, in_specs=[anywhere] * 3, o...  1.81 us

profile of v3, /device:TPU:0, one launch (start us, length us, event | category | flops | bytes accessed | tf_op | source)
XLA Modules:
  0.0 42.4 jit_solution(3026249301075890523)
XLA Ops:
  1.3 39.3 %shard_map.103 = (bf16[128,256]{1,0:T(8,128)(2,1)}, f32[128,256]{1,0:T(8,128)}, f32[256,256]{1,0:T(8,128)}) custom-call(bf16[128,256]{1,0:T(8,128)(2,1)} %feat_hbm.1, bf16[1,1,32,128,128]{4,3,2,1,0:T(8,128)(2,1)} %tiles_hbm.1, s32[1,1,32]{2,1,0:T(1,128)} %row_ids_hbm.1, s32[1,1,32]{2,1,0:T(1,128)} %col_ids_hbm.1, s32[1,1]{1,0:T(1,128)S(6)} %copy.11.live, ...), custom_call_target="tpu_custom_call" | custom-call | tf_op jit(solution)/shard_map/pallas_call | solution.py:416
  40.6 1.8 %shard_map.104 = (bf16[128,256]{1,0:T(8,128)(2,1)}, f32[128,256]{1,0:T(8,128)}, f32[256,256]{1,0:T(8,128)}) custom-call(bf16[128,256]{1,0:T(8,128)(2,1)} %get-tuple-element.6.refs_0_, f32[128,256]{1,0:T(8,128)} %get-tuple-element.7.refs_1_, f32[256,256]{1,0:T(8,128)} %get-tuple-element.8.refs_2_), custom_call_target="tpu_custom_call" | custom-call | tf_op jit(solution)/shard_map/pallas_call | solution.py:463

commit v4 on v3

--- a/solution.py
+++ b/solution.py
@@ -29,9 +29,9 @@
     feat_hbm, tiles_hbm, row_ids_hbm, col_ids_hbm, live, weight_hbm, bias_hbm, cot_hbm,
     out_hbm, grad_feat_hbm, grad_w_hbm,
     feat, row_ids, col_ids, weight, bias, cot, out, grad_feat, grad_w,
-    tiles, adj, adj_t, gathered, acc, part_send, part_recv, grads,
+    tiles, adj, adj_t, gathered, acc, chip_in, part_send, part_recv, grads,
     y_out, y_in, keep, z_out, z_in, w_out, w_in, w_sum, w_cols, w_all,
-    load_sems, store_sems, tile_sem, xz_send, xy_send, x_recv, p_send, p_recv, g_send, g_recv,
+    load_sems, store_sems, tile_sem, xz_send, xy_send, x_recv, p1_send, p1_recv, p_send, p_recv, g_send, g1_send, g_recv,
     by_send, by_recv, bz_send, bz_recv,
     w1_send, w1_recv, w2_send, w2_recv, w3_send, w3_recv,
 ):
@@ -48,6 +48,14 @@
 
     def col_peer(k):
         return lax.rem(j + k, n_col)
+
+    pairs = n_col // 2
+    pair = j // 2
+    core = j % 2
+    partner = 2 * pair + 1 - core
+
+    def pair_peer(k):
+        return lax.rem(pair + k, pairs)
 
     def y_peer(k):
         return lax.rem(y + k, inner)
@@ -218,25 +226,41 @@
             add_block(block, gathered[block], False)
         loop(inner - 1, take_features)
 
+    def p1_copy(pair):
+        to = 2 * pair + 1 - core
+        return send(
+            acc.at[pl.ds(pl.multiple_of(to * size, size), size), :], chip_in.at[pair],
+            p1_send.at[pair], p1_recv.at[pair], "col", partner,
+        )
+
     def p_copy(to, sender):
         return send(
-            part_send.at[to], part_recv.at[sender], p_send.at[to], p_recv.at[sender], "col", to
-        )
+            part_send.at[to], part_recv.at[sender], p_send.at[to], p_recv.at[sender],
+            "col", 2 * to + core,
+        )
+
+    def mine(pair):
+        return pl.ds(pl.multiple_of((2 * pair + core) * size, size), size)
+
+    loop(pairs, lambda k: p1_copy(pair_peer(k + 1)).start())
 
     def send_partial(k):
-        to = col_peer(k + 1)
-        part_send[to] = acc[pl.ds(pl.multiple_of(to * size, size), size), :].astype(BF16)
-        p_copy(to, j).start()
-
-    loop(n_col - 1, send_partial)
-    acc_own = pl.ds(pl.multiple_of(j * size, size), size)
+        to = pair_peer(k + 1)
+        p1_copy(to).wait_recv()
+        part_send[to] = (acc[mine(to), :] + chip_in[to]).astype(BF16)
+        p_copy(to, pair).start()
+
+    loop(pairs - 1, send_partial)
+    p1_copy(pair).wait_recv()
+    acc_own = mine(pair)
+    acc[acc_own, :] += chip_in[pair]
 
     def take_partial(k):
-        sender = lax.rem(j + n_col - 1 - k, n_col)
+        sender = pair_peer(pairs - 1 - k)
         p_copy(sender, sender).wait_recv()
         acc[acc_own, :] += part_recv[sender].astype(F32)
 
-    loop(n_col - 1, take_partial)
+    loop(pairs - 1, take_partial)
 
     aggregate = acc[acc_own, :].astype(BF16)
     for load in loads[3:]:
@@ -323,7 +347,7 @@
         z_out[block_z] = keep[block_z].astype(BF16)
         bz_copy(block_z, z).start()
 
-    for block_z in z_far_first[:2]:
+    for block_z in z_far_first:
         pass_back(block_z)
 
     w_cols[j] = w_sum[...]
@@ -342,8 +366,6 @@
 
     loop(n_row - 1, lambda k: w3_copy(row_peer(k + 1), i).start())
 
-    for block_z in z_far_first[2:]:
-        pass_back(block_z)
     add_back(z)
     total = keep[z]
     for block_z in z_near_first:
@@ -366,11 +388,20 @@
 
     def col_sent(k):
         to = col_peer(k + 1)
-        p_copy(to, j).wait_send()
+        w2_copy(to, j).wait_send()
         g_copy(to, j).wait_send()
-        w2_copy(to, j).wait_send()
 
     loop(n_col - 1, col_sent)
+
+    def pair_sent(k):
+        to = pair_peer(k + 1)
+        p_copy(to, pair).wait_send()
+
+    def chip_sent(k):
+        p1_copy(k).wait_send()
+
+    loop(pairs - 1, pair_sent)
+    loop(pairs, chip_sent)
     for block_z in z_near_first:
         bz_copy(block_z, z).wait_send()
     for block_z in (z,) + z_near_first:
@@ -407,6 +438,7 @@
     anywhere = pl.BlockSpec(memory_space=pl.ANY)
     row_dma = pltpu.SemaphoreType.DMA((n_row,))
     col_dma = pltpu.SemaphoreType.DMA((n_col,))
+    pair_dma = pltpu.SemaphoreType.DMA((n_col // 2,))
     z_dma = pltpu.SemaphoreType.DMA((outer,))
     out_shape = (
         jax.ShapeDtypeStruct((size, out_width), BF16),
@@ -433,8 +465,9 @@
             pltpu.VMEM((n_row, size, rows) if pre_transpose else (1, 16, 128), BF16),
             pltpu.VMEM((n_row, size, width), BF16),
             pltpu.VMEM((rows, width), F32),
-            pltpu.VMEM((n_col, size, width), BF16),
-            pltpu.VMEM((n_col, size, width), BF16),
+            pltpu.VMEM((n_col // 2, size, width), F32),
+            pltpu.VMEM((n_col // 2, size, width), BF16),
+            pltpu.VMEM((n_col // 2, size, width), BF16),
             pltpu.VMEM((n_col, size, width), BF16),
             pltpu.VMEM((n_row, size, width), BF16),
             pltpu.VMEM((n_row, size, width), BF16),
@@ -449,7 +482,8 @@
             pltpu.SemaphoreType.DMA((6,)),
             pltpu.SemaphoreType.DMA((3,)),
             pltpu.SemaphoreType.DMA,
-            z_dma, row_dma, row_dma, col_dma, col_dma, col_dma, col_dma,
+            z_dma, row_dma, row_dma, pair_dma, pair_dma, pair_dma, pair_dma,
+            col_dma, pair_dma, col_dma,
             row_dma, row_dma, z_dma, z_dma,
             row_dma, row_dma, col_dma, col_dma, row_dma, row_dma,
         ],

time: 42.5 us -> 42.3 us (level)
  no operation moved by 1% of the time
where the time goes in v4:
time: 42.3 us; the launch traced here: 42.1 us
  Pallas kernels  40.8 us (96%)
  between operations  1.29 us (3%)
    pallas_call x1, Pallas kernels, shards(): pl.pallas_call(functools.partial(kernel, n_row, n_col, outer, pre_transpo...  39 us
    pallas_call x1, Pallas kernels, shards(): pl.pallas_call(hand_over, out_shape=out_shape, in_specs=[anywhere] * 3, o...  1.81 us

profile of v4, /device:TPU:0, one launch (start us, length us, event | category | flops | bytes accessed | tf_op | source)
XLA Modules:
  0.0 42.1 jit_solution(11406620872183853488)
XLA Ops:
  1.3 39.0 %shard_map.103 = (bf16[128,256]{1,0:T(8,128)(2,1)}, f32[128,256]{1,0:T(8,128)}, f32[256,256]{1,0:T(8,128)}) custom-call(bf16[128,256]{1,0:T(8,128)(2,1)} %feat_hbm.1, bf16[1,1,32,128,128]{4,3,2,1,0:T(8,128)(2,1)} %tiles_hbm.1, s32[1,1,32]{2,1,0:T(1,128)} %row_ids_hbm.1, s32[1,1,32]{2,1,0:T(1,128)} %col_ids_hbm.1, s32[1,1]{1,0:T(1,128)S(6)} %copy.11.live, ...), custom_call_target="tpu_custom_call" | custom-call | tf_op jit(solution)/shard_map/pallas_call | solution.py:448
  40.3 1.8 %shard_map.104 = (bf16[128,256]{1,0:T(8,128)(2,1)}, f32[128,256]{1,0:T(8,128)}, f32[256,256]{1,0:T(8,128)}) custom-call(bf16[128,256]{1,0:T(8,128)(2,1)} %get-tuple-element.6.refs_0_, f32[128,256]{1,0:T(8,128)} %get-tuple-element.7.refs_1_, f32[256,256]{1,0:T(8,128)} %get-tuple-element.8.refs_2_), custom_call_target="tpu_custom_call" | custom-call | tf_op jit(solution)/shard_map/pallas_call | solution.py:497
